TPU v7x, 32 devices: a whole 2x2x4 slice. The times are simulated.
32 devices in a mesh: prow: 4 (over y, x), pcol: 8 (over z, core).
Axes of the slice: x: 2, y: 2, z: 4, core: 2. Of those that a mesh axis runs over, the one named last changes fastest.
Arguments:
- left_factor: bfloat16 [16, 16, 2048, 128], P('prow', 'pcol'), may hold values from -0.8984375 to 0.8984375
- right_factor: bfloat16 [16, 16, 2048, 128], P('prow', 'pcol'), may hold values from -0.8984375 to 0.8984375
- pivot_left: bfloat16 [16, 2048, 128], P('pcol', 'prow'), may hold values from -0.8984375 to 0.8984375
- pivot_right: bfloat16 [16, 2048, 128], P('pcol', 'prow'), may hold values from -0.8984375 to 0.8984375
- target_left: bfloat16 [2048, 16, 128], P('pcol', 'prow'), may hold values from -6 to 6
- target_right: bfloat16 [2048, 16, 128], P('pcol', 'prow'), may hold values from -6 to 6
- probe: bfloat16 [2048, 128], P('prow'), may hold values from -6 to 6
- ranks: int32 [16, 16], P('prow', 'pcol'), may hold values from 16 to 128
Outputs:
- basis: float32 [2048, 16, 128], P('pcol', 'prow')
- coefficient: float32 [2048, 16, 128], P('pcol', 'prow')
All inputs are finite; a program needn't handle non-finite values.
Results may differ from a plain program's by a relative error of at most 0.0038.
Values may be sent and summed in bfloat16 or wider, within the bound.
A program may use at most 64 MiB of HBM per device.

v0:
```python
import jax
import jax.numpy as jnp
from jax import lax
from jax.sharding import PartitionSpec as P

exact_mode = lax.Precision.HIGHEST


def solve_rows(lower_factor, samples):
    stacked = jnp.transpose(samples, (1, 0, 2))
    solved = lax.linalg.triangular_solve(
        lower_factor, stacked, left_side=False, lower=True, transpose_a=True
    )
    return jnp.transpose(solved, (1, 0, 2))


def per_device(
    left_factor, right_factor, pivot_left, pivot_right, target_left, target_right, probe, ranks
):
    pivot_whole, pivot_other, probe_whole = (
        lax.all_gather(pivot_left, "prow", axis=1, tiled=True),
        lax.all_gather(pivot_right, "prow", axis=1, tiled=True),
        lax.all_gather(probe, "prow", axis=0, tiled=True),
    )
    order_full = left_factor.shape[2]
    rank_span = left_factor.shape[3]
    row_count = target_left.shape[0]
    first_row = lax.axis_index("pcol") * row_count
    probe_slice = lax.dynamic_slice_in_dim(probe_whole, first_row, row_count, 0)
    sample_part = jnp.einsum(
        "bir,bs->irs", target_right, probe_slice, preferred_element_type=jnp.float32
    )
    target_sample = lax.psum(sample_part, "pcol")
    pivot_sample = jnp.einsum(
        "jbr,bs->jrs", pivot_whole, probe_whole, preferred_element_type=jnp.float32
    )
    rank_index = lax.broadcasted_iota(jnp.int32, ranks.shape + (rank_span,), 2)
    rank_mask = (rank_index < ranks[:, :, None]).astype(jnp.float32)
    coupling = jnp.einsum(
        "ijbr,jbs->ijrs", right_factor, pivot_other, preferred_element_type=jnp.float32
    )
    coupling = coupling * rank_mask[:, :, :, None]
    weights = jnp.einsum("ijrs,jst->ijrt", coupling, pivot_sample, precision=exact_mode).astype(
        jnp.bfloat16
    )
    target_term = jnp.einsum(
        "bis,ist->bit", target_left.astype(jnp.float32), target_sample, precision=exact_mode
    )
    partial_all = -jnp.einsum(
        "ijbr,ijrt->bit", left_factor, weights, preferred_element_type=jnp.float32
    )
    own_rows = lax.dynamic_slice_in_dim(partial_all, first_row, row_count, 0) + target_term
    partial_all = lax.dynamic_update_slice_in_dim(partial_all, own_rows, first_row, 0)
    samples_all = lax.psum(partial_all, "pcol")
    gram_matrix = (
        jnp.einsum("bir,bis->irs", samples_all, samples_all, precision=exact_mode) / order_full
    )
    lower_factor = jnp.linalg.cholesky(gram_matrix)
    basis_all = solve_rows(lower_factor, samples_all)
    basis_full = basis_all.astype(jnp.bfloat16)
    basis_rows = lax.dynamic_slice_in_dim(basis_all, first_row, row_count, 0)
    basis_half = basis_rows.astype(jnp.bfloat16)
    correlation = jnp.einsum(
        "ijbr,bit->ijrt", left_factor, basis_full, preferred_element_type=jnp.float32
    )
    reduced = jnp.einsum("ijrs,ijrt->ijst", coupling, correlation, precision=exact_mode).astype(
        jnp.bfloat16
    )
    correlation_part = jnp.einsum(
        "bis,bit->ist", target_left, basis_half, preferred_element_type=jnp.float32
    )
    target_correlation = lax.psum(correlation_part, "pcol").astype(jnp.bfloat16)
    projected = lax.psum_scatter(
        -jnp.einsum("jbs,ijst->bit", pivot_whole, reduced, preferred_element_type=jnp.float32),
        "pcol",
        scatter_dimension=0,
        tiled=True,
    )
    own_term = jnp.einsum(
        "bis,ist->bit", target_right, target_correlation, preferred_element_type=jnp.float32
    )
    coefficient = (projected + own_term) / order_full
    return (basis_rows, coefficient)


def solution(mesh):
    in_specs = (
        P("prow", "pcol", None, None),
        P("prow", "pcol", None, None),
        P("pcol", "prow", None),
        P("pcol", "prow", None),
        P("pcol", "prow", None),
        P("pcol", "prow", None),
        P("prow", None),
        P("prow", "pcol"),
    )
    out_specs = (P("pcol", "prow", None), P("pcol", "prow", None))
    return jax.shard_map(
        per_device, mesh=mesh, in_specs=in_specs, out_specs=out_specs, check_vma=False
    )
```

profile of v0, /device:TPU:0, one launch (start us, length us, event | category | flops | bytes accessed | tf_op | source)
XLA Modules:
  0.0 351.0 jit_solution(17695001845141347248)
XLA Ops:
  8.0 0.0 copy-start
  8.0 0.0 all-gather.3.cloned.1.call-start
  8.1 0.7 all-gather.3.cloned.1.call-update
  8.7 0.0 all-gather.5.cloned.1.call-start
  8.8 1.8 copy.20
  10.6 0.0 all-gather.5.cloned.1.call-update
  10.6 0.0 all-reduce.4.cloned.1.call-start
  10.7 11.8 %all_gather.10 = bf16[2048,128]{1,0:T(8,128)(2,1)S(1)} all-gather(bf16[512,128]{1,0:T(8,128)(2,1)} %param.14), channel_id=1, replica_groups=mesh['prow'=4,'pcol'=8] {'prow'}, dimensions={0}, use_global_device_ids=true | all-gather | bytes 655360 | tf_op jit(solution)/shard_map/all_gather | solution.py:23
  22.5 1.9 convolution_bitcast_fusion.2
  24.4 0.0 all-reduce.4.cloned.1.call-update
  24.4 0.0 all-reduce.6.cloned.1.call-start
  24.5 0.8 fusion.35
  25.2 15.0 %all-gather.3.cloned.1.call-done = bf16[2,2048,128]{2,1,0:T(8,128)(2,1)} async-done(((bf16[2,512,128]{2,1,0:T(8,128)(2,1)}), bf16[2,2048,128]{2,1,0:T(8,128)(2,1)}) %all-gather.3.cloned.1.call-update) | async-done | bytes 1048592 | tf_op jit(solution)/shard_map/all_gather | solution.py:21
  40.2 1.7 convolution_bitcast_fusion.3
  41.9 27.4 %all-gather.5.cloned.1.call-done = bf16[2,2048,128]{1,2,0:T(8,128)(2,1)} async-done(((bf16[2,512,128]{1,2,0:T(8,128)(2,1)}), bf16[2,2048,128]{1,2,0:T(8,128)(2,1)}) %all-gather.5.cloned.1.call-update) | async-done | bytes 1048592 | tf_op jit(solution)/shard_map/all_gather | solution.py:22
  69.3 3.4 fusion.15
  72.7 0.6 fusion.18
  73.3 0.0 copy-done.3
  73.3 1.5 bitcast_negate_fusion.1
  74.8 2.0 copy-done.2
  76.8 1.9 copy.63
  78.7 0.9 all-reduce.4.cloned.1.call-done
  79.6 2.4 fusion.14
  82.0 0.0 all-reduce.6.cloned.1.call-update
  82.0 0.0 reduce-scatter.2.cloned.1.call-start
  82.1 95.5 %all-reduce.6.cloned.1.call-done = f32[2048,4,128]{0,2,1:T(8,128)} async-done(((f32[2048,4,128]{0,2,1:T(8,128)}), f32[2048,4,128]{0,2,1:T(8,128)}) %all-reduce.6.cloned.1.call-update) | async-done | bytes 4194320 | tf_op jit(solution)/shard_map/psum | solution.py:54
  177.5 7.4 %fusion.37 = f32[4,128,128]{2,1,0:T(8,128)S(1)} fusion(f32[2048,4,128]{0,2,1:T(8,128)} %all-reduce.6.cloned.1.call-done), kind=kOutput, calls=%fused_computation.51 | convolution fusion | flops 1610612736 | bytes 4456448 | tf_op jit(solution)/shard_map/bir,bis->irs/dot_general | solution.py:56
  184.9 0.1 copy.24
  185.1 47.1 %custom-call.7 = f32[4,128,128]{2,1,0:T(8,128)S(1)} custom-call(f32[4,128,128]{2,1,0:T(8,128)S(1)} %fusion.26), custom_call_target="Cholesky" | custom-call | tf_op jit(solution)/shard_map/jit(cholesky)/cholesky | solution.py:58
  232.2 0.1 compare_reduce_fusion
  232.4 0.1 select_bitcast_fusion
  232.5 39.3 %custom-call.8 = f32[4,1,128,128]{2,3,1,0:T(8,128)S(1)} custom-call(f32[4,1,128,128]{3,2,1,0:T(8,128)S(1)} %select_bitcast_fusion), custom_call_target="InvertDiagBlocksLowerTriangular" | custom-call | tf_op jit(solution)/shard_map/triangular_solve | solution.py:11
  271.8 0.0 copy-start.4
  271.8 8.8 %fusion.1 = f32[4,2048,128]{2,1,0:T(8,128)S(1)} fusion(f32[2048,4,128]{0,2,1:T(8,128)} %all-reduce.6.cloned.1.call-done, f32[4,1,128,128]{2,3,1,0:T(8,128)S(1)} %custom-call.8), kind=kOutput, calls=%fused_computation.2 | convolution fusion | flops 1610612736 | bytes 8650752 | tf_op jit(solution)/shard_map/triangular_solve | solution.py:11
  280.7 0.9 fusion.5
  281.6 1.0 copy-done.1
  282.6 0.4 copy.61
  283.0 1.2 convolution_convert_fusion.1
  284.2 2.7 fusion
  287.0 0.0 reduce-scatter.2.cloned.1.call-update
  287.0 1.1 dynamic-slice_bitcast_fusion
  288.1 1.1 copy.28
  289.2 0.3 convolution_bitcast_fusion.1
  289.5 37.3 %all-reduce.7 = bf16[4,128,128]{1,2,0:T(8,128)(2,1)S(1)} all-reduce(f32[4,128,128]{1,2,0:T(8,128)S(1)} %convolution_bitcast_fusion.1), channel_id=1, replica_groups=mesh['prow'=4,'pcol'=8] {'pcol'}, use_global_device_ids=true, to_apply=%region_5.6 | all-reduce | flops 65536 | bytes 393216 | tf_op jit(solution)/shard_map/psum | solution.py:72
  326.8 14.3 %reduce-scatter.2.cloned.1.call-done = f32[256,4,128]{0,2,1:T(8,128)} async-done(((f32[2048,4,128]{0,2,1:T(8,128)}), f32[256,4,128]{0,2,1:T(8,128)}) %reduce-scatter.2.cloned.1.call-update) | async-done | bytes 524304 | tf_op jit(solution)/shard_map/reduce_scatter | solution.py:73
  341.2 0.0 copy-done.6
  341.2 1.3 fusion.12
  342.4 1.0 copy.29
  (12 shorter events, 0.1 us)
Async XLA Ops:
  8.0 71.6 %copy-start = (bf16[256,4,128]{2,1,0:T(4,128)(2,1)S(1)}, bf16[256,4,128]{2,1,0:T(4,128)(2,1)}, u32[]{:S(2)}) copy-start(bf16[256,4,128]{2,1,0:T(4,128)(2,1)} %param.12) | copy-start | bytes 786436
  8.0 32.2 %all-gather.3.cloned.1.call-start = ((), (), s32[]{:S(2)}) async-start(), calls=%async_computation.1 | async-start | bytes 1310720 | tf_op jit(solution)/shard_map/all_gather | solution.py:21
  8.7 60.5 %all-gather.5.cloned.1.call-start = ((), (), s32[]{:S(2)}) async-start(), calls=%async_computation.2 | async-start | bytes 1310720 | tf_op jit(solution)/shard_map/all_gather | solution.py:22
  10.6 69.0 %all-reduce.4.cloned.1.call-start = ((), (), s32[]{:S(2)}) async-start(), calls=%async_computation.3 | async-start | bytes 524288 | tf_op jit(solution)/shard_map/psum | solution.py:33
  24.4 153.1 %all-reduce.6.cloned.1.call-start = ((), (), s32[]{:S(2)}) async-start(), calls=%async_computation.4 | async-start | bytes 8388608 | tf_op jit(solution)/shard_map/psum | solution.py:54
  69.3 4.1 %copy-start.3 = (bf16[4,2,2048,128]{3,2,1,0:T(8,128)(2,1)S(1)}, bf16[4,2,2048,128]{3,2,1,0:T(8,128)(2,1)}, u32[]{:S(2)}) copy-start(bf16[4,2,2048,128]{3,2,1,0:T(8,128)(2,1)} %param.8) | copy-start | bytes 12582916
  74.8 2.0 copy-start.2
  82.0 259.2 %reduce-scatter.2.cloned.1.call-start = ((), (), s32[]{:S(2)}) async-start(), calls=%async_computation.5 | async-start | bytes 4718592 | tf_op jit(solution)/shard_map/reduce_scatter | solution.py:73
  271.8 8.9 %copy-start.4 = (bf16[4,2,2048,128]{3,2,1,0:T(8,128)(2,1)S(1)}, bf16[4,2,2048,128]{3,2,1,0:T(8,128)(2,1)}, u32[]{:S(2)}) copy-start(bf16[4,2,2048,128]{3,2,1,0:T(8,128)(2,1)} %param.8) | copy-start | bytes 12582916
  280.7 1.9 copy-start.1
  280.7 3.6 %copy-start.5 = (bf16[2,2048,128]{2,1,0:T(8,128)(2,1)S(1)}, bf16[2,2048,128]{2,1,0:T(8,128)(2,1)}, u32[]{:S(2)}) copy-start(bf16[2,2048,128]{2,1,0:T(8,128)(2,1)} %all-gather.3.cloned.1.call-done) | copy-start | bytes 3145732
  286.9 54.2 %copy-start.6 = (bf16[256,4,128]{2,1,0:T(4,128)(2,1)S(1)}, bf16[256,4,128]{2,1,0:T(4,128)(2,1)}, u32[]{:S(2)}) copy-start(bf16[256,4,128]{2,1,0:T(4,128)(2,1)} %param.13) | copy-start | bytes 786436
Sparse Core Ops, SparseCore 0:
  10.8 29.3 all-gather.2
  42.7 26.4 all-gather.4
Sparse Core Ops, SparseCore 1:
  24.5 55.1 all-reduce.3
  82.1 95.4 all-reduce.5
  287.1 54.0 reduce-scatter.1
where the time goes:
time: 351 us
  waiting for transfers between devices  154 us (44%)
  other arithmetic  87.5 us (25%)
  blocking collectives  49.1 us (14%)
  matrix products  34.1 us (10%)
  between operations  15.9 us (5%)
  local copies, waits for them, and re-layouts  10.5 us (3%)
    psum x1, waiting for transfers between devices, per_device(): samples_all = lax.psum(partial_all, 'pcol')  95.5 us
    another operation x4, other arithmetic, per_device(): lower_factor = jnp.linalg.cholesky(gram_matrix)  47.3 us
    another operation x3, other arithmetic, solve_rows(): lax.linalg.triangular_solve(lower_factor, stacked, left_side=False, lower...  39.4 us
    psum x1, blocking collectives, per_device(): target_correlation = lax.psum(correlation_part, 'pcol').astype(jnp.bfloat16)  37.3 us
    all_gather x1, waiting for transfers between devices, per_device(): lax.all_gather(pivot_right, 'prow', axis=1, tiled=True)  27.4 us
    all_gather x1, waiting for transfers between devices, per_device(): lax.all_gather(pivot_left, 'prow', axis=1, tiled=True)  15 us
    reduce_scatter x1, waiting for transfers between devices, per_device(): lax.psum_scatter(-jnp.einsum('jbs,ijst->bit', pivot_whole, reduced, prefe...  14.3 us
    all_gather x1, blocking collectives, per_device(): lax.all_gather(probe, 'prow', axis=0, tiled=True)  11.8 us
  transfers between devices with their start and end apart: 5, of which 5 were waited for; matrix products, arithmetic and copies ran while one was open for 5% of the time, Pallas kernels for 0%

commit v1 on v0

v1 whole, which is shorter than its diff:
```python
import functools

import jax
import jax.numpy as jnp
from jax import lax
from jax.experimental import pallas as pl
from jax.experimental.pallas import tpu as pltpu
from jax.sharding import PartitionSpec as P

EXACT = lax.Precision.HIGHEST
MESH = pl.DeviceIdType.MESH
F32 = jnp.float32
BF16 = jnp.bfloat16


def dot(a, b, ca, cb, precision=None):
    return lax.dot_general(
        a, b, (((ca,), (cb,)), ((), ())), precision=precision, preferred_element_type=F32
    )


def inverse_factor(gram_ref, eye_ref, out_ref, start, tiles, span, block):
    row_in_block = lax.broadcasted_iota(jnp.int32, (tiles, block, 1), 1)
    rows = lax.broadcasted_iota(jnp.int32, (tiles, span, span), 1)
    columns = lax.broadcasted_iota(jnp.int32, (tiles, span, span), 2)
    group = slice(start, start + tiles)
    eye_ref[group] = (rows == columns).astype(F32)
    for first in range(0, span, block):
        g = gram_ref[group, first : first + block, :]
        e = eye_ref[group, first : first + block, :]
        for k in range(block):
            column = jnp.broadcast_to(
                g[:, :, first + k : first + k + 1], (tiles, block, span)
            )
            pivot = column[:, k : k + 1, :]
            scale = lax.rsqrt(pivot)
            scale = scale * (1.5 - 0.5 * pivot * scale * scale)
            g_row = g[:, k : k + 1, :] * scale
            e_row = e[:, k : k + 1, :] * scale
            factor = column * scale
            below = row_in_block > k
            here = row_in_block == k
            g = jnp.where(below, g - factor * g_row, jnp.where(here, g_row, g))
            e = jnp.where(below, e - factor * e_row, jnp.where(here, e_row, e))
        out_ref[group, first : first + block, :] = e
        if first + block < span:
            for i in range(tiles):
                gi, ei = g[i], e[i]
                turned = gi.T
                gram_ref[start + i] = gram_ref[start + i] - dot(turned, gi, 1, 0, EXACT)
                eye_ref[start + i] = eye_ref[start + i] - dot(turned, ei, 1, 0, EXACT)


def kernel(
    n_p, n_q,
    left_hbm, right_hbm, pivot_left, pivot_right, target_left, target_right, probe, ranks_hbm,
    basis, coefficient,
    ranks, left, right, left_full, right_full, probe_block, coupling, weights,
    ps_part, ps_recv, ps_sum,
    t_part, t_sib, t_chip, t_z, t_own, t_other, t_full,
    acc, sib_send, sib_recv, z_send, z_recv,
    samples, samples_full, raw,
    c_part, c_sib, c_chip, c_z, c_own, c_other, c_full,
    gram, eye, inverse, reduced,
    sib_send2, sib_recv2, z_send2, z_recv2,
    local_sem, probe_s, probe_r, pr_s, pr_r, ps_s, ps_r, pl_s, pl_r,
    ts_s, ts_r, tz_s, tz_r, to_s, to_r,
    ss_s, ss_r, sz_s, sz_r,
    gz_s, gz_r, gs_s, gs_r,
    cs_s, cs_r, cz_s, cz_r, co_s, co_r,
    fs_s, fs_r, fz_s, fz_r,
):
    p = lax.axis_index("prow")
    q = lax.axis_index("pcol")
    n_z = n_q // 2
    z = q // 2
    c = q % 2
    sibling = (p, q + 1 - 2 * c)
    ni, nj, order, span = left.shape
    rp = probe.shape[0]
    rq = target_left.shape[1]
    half = ni // 2

    def peer_p(d):
        return (lax.rem(p + d, n_p), q)

    def peer_z(d):
        return (p, lax.rem(z + d, n_z) * 2 + c)

    def row_block(index, size):
        return pl.ds(pl.multiple_of(index * size, size), size)

    def remote(src, dst, s, r, where):
        return pltpu.make_async_remote_copy(
            src_ref=src, dst_ref=dst, send_sem=s, recv_sem=r, device_id=where, device_id_type=MESH
        )

    right_copy = pltpu.make_async_copy(right_hbm, right, local_sem.at[0])
    left_copy = pltpu.make_async_copy(left_hbm, left, local_sem.at[1])
    right_copy.start()
    left_copy.start()
    ranks_copy = pltpu.make_async_copy(ranks_hbm, ranks, local_sem.at[2])
    ranks_copy.start()

    barrier = pltpu.get_barrier_semaphore()
    partners = [peer_p(d) for d in range(1, n_p)] + [peer_z(d) for d in range(1, n_z)] + [sibling]
    for partner in partners:
        pl.semaphore_signal(barrier, inc=1, device_id=partner, device_id_type=MESH)
    pl.semaphore_wait(barrier, len(partners))

    owner = (q * rq) // rp

    def mine():
        return pl.ds(pl.multiple_of(lax.rem(q * rq, rp), rq), rq)

    @pl.when(p == owner)
    def _():
        for d in range(1, n_p):
            remote(probe.at[mine()], probe_block, probe_s.at[d - 1], probe_r, peer_p(d)).start()
        probe_block[...] = probe[mine(), :]

    pr_copies = [
        remote(pivot_right, right_full.at[:, row_block(p, rp), :], pr_s.at[d - 1], pr_r.at[d - 1], peer_p(d))
        for d in range(1, n_p)
    ]
    for copy in pr_copies:
        copy.start()
    for j in range(nj):
        ps_part[j] = dot(pivot_left[j], probe[...], 0, 0)
    ps_copies = [
        remote(ps_part, ps_recv.at[d - 1], ps_s.at[d - 1], ps_r.at[d - 1], peer_p(d))
        for d in range(1, n_p)
    ]
    for copy in ps_copies:
        copy.start()
    pl_copies = [
        remote(pivot_left, left_full.at[:, row_block(p, rp), :], pl_s.at[d - 1], pl_r.at[d - 1], peer_p(d))
        for d in range(1, n_p)
    ]
    @pl.when(p != owner)
    def _():
        remote(probe.at[mine()], probe_block, probe_s.at[0], probe_r, peer_p(1)).wait_recv()

    for i in range(ni):
        t_part[i] = dot(target_right[i], probe_block[...], 0, 0)

    def half_of(core):
        return pl.ds(core * half, half)

    t_first = remote(t_part.at[half_of(1 - c)], t_sib, ts_s, ts_r, sibling)
    t_first.start()
    right_copy.wait()

    def couple(rows, chunk_ref):
        def body(n, carry):
            i, j = n // nj, n % nj
            coupling[i, j] += dot(chunk_ref[j], right[i, j, rows, :], 0, 0)
            return carry
        lax.fori_loop(0, ni * nj, body, 0)

    coupling[...] = jnp.zeros_like(coupling)
    couple(row_block(p, rp), pivot_right)

    t_first.wait()
    t_chip[...] = t_part[half_of(c)] + t_sib[...]
    t_second = [
        remote(t_chip, t_z.at[d - 1], tz_s.at[d - 1], tz_r.at[d - 1], peer_z(d)) for d in range(1, n_z)
    ]
    for copy in t_second:
        copy.start()

    for d in range(1, n_p):
        pr_copies[d - 1].wait()
        rows = row_block(lax.rem(p - d + n_p, n_p), rp)
        couple(rows, right_full.at[:, rows, :])
    total = ps_part[...]
    for d in range(1, n_p):
        ps_copies[d - 1].wait()
        total = total + ps_recv[d - 1]
    ps_sum[...] = total
    for copy in pl_copies:
        copy.start()
    left_copy.wait()
    ranks_copy.wait()

    sib_copies = lambda i: remote(sib_send.at[i], sib_recv.at[i], ss_s.at[i], ss_r.at[i], sibling)
    z_copies = lambda i, d: remote(
        z_send.at[i, d - 1], z_recv.at[i, d - 1], sz_s.at[i, d - 1], sz_r.at[i, d - 1], peer_z(d)
    )
    lane = lax.broadcasted_iota(jnp.int32, (span, span), 1)

    def update(i, carry):
        for j in range(nj):
            masked = jnp.where(lane < ranks[i, j], coupling[i, j], 0.0)
            coupling[i, j] = masked
            weights[j] = dot(masked.T, ps_sum[j], 1, 0, EXACT).astype(BF16)

        def rows_of(zz, inner):
            for parity in range(2):
                core = c if parity == 0 else 1 - c
                rows = row_block(2 * zz + core, rq)
                part = dot(left[i, 0, rows, :], weights[0], 1, 0)
                for j in range(1, nj):
                    part = part + dot(left[i, j, rows, :], weights[j], 1, 0)
                if parity == 0:
                    acc[i, zz] = part
                else:
                    sib_send[i, zz] = part.astype(BF16)
            return inner

        lax.fori_loop(0, n_z, rows_of, 0)
        sib_copies(i).start()
        return carry

    lax.fori_loop(0, ni, update, 0)

    def forward(i, carry):
        sib_copies(i).wait()
        for d in range(1, n_z):
            to = lax.rem(z + d, n_z)
            z_send[i, d - 1] = (acc[i, to] + sib_recv[i, to].astype(F32)).astype(BF16)
            z_copies(i, d).start()
        return carry

    def sent(i, carry):
        for d in range(1, n_z):
            z_copies(i, d).wait_send()
        return carry

    lax.fori_loop(0, half, forward, 0)

    def finish(second, chip, arrived, own, other, whole, s, r):
        for copy in second:
            copy.wait()
        value = chip[...].astype(F32)
        for d in range(1, n_z):
            value = value + arrived[d - 1].astype(F32)
        own[...] = value
        last = remote(own, other, s, r, sibling)
        last.start()
        last.wait()
        whole[half_of(c)] = own[...]
        whole[half_of(1 - c)] = other[...]

    finish(t_second, t_chip, t_z, t_own, t_other, t_full, to_s, to_r)
    lax.fori_loop(0, half, sent, 0)
    lax.fori_loop(half, ni, forward, 0)

    gather_z = lambda i, d: remote(
        samples_full.at[i, row_block(q, rq), :], samples_full.at[i, row_block(q, rq), :],
        gz_s.at[i, d - 1], gz_r.at[i, d - 1], peer_z(d),
    )

    def gather_sib(i, d):
        rows = row_block(2 * lax.rem(z - d + n_z, n_z) + c, rq)
        block = samples_full.at[i, rows, :]
        return remote(block, block, gs_s.at[i, d], gs_r.at[i, d], sibling)

    def sample(i, carry):
        value = dot(target_left[i].astype(F32), t_full[i], 1, 0, EXACT)
        value = value - acc[i, z] - sib_recv[i, z].astype(F32)
        for d in range(1, n_z):
            z_copies(i, d).wait_recv()
            value = value - z_recv[i, d - 1].astype(F32)
        samples[i] = value
        rounded = value.astype(BF16)
        samples_full[i, row_block(q, rq), :] = rounded
        for d in range(1, n_z):
            gather_z(i, d).start()
        gather_sib(i, 0).start()
        c_part[i] = dot(rounded, target_left[i], 0, 0)
        return carry

    lax.fori_loop(0, ni, sample, 0)
    lax.fori_loop(half, ni, sent, 0)
    c_first = remote(c_part.at[half_of(1 - c)], c_sib, cs_s, cs_r, sibling)
    c_first.start()

    def relay(i, carry):
        for d in range(1, n_z):
            gather_z(i, d).wait()
            gather_sib(i, d).start()
        return carry

    c_first.wait()
    c_chip[...] = (c_part[half_of(c)] + c_sib[...]).astype(BF16)
    c_second = [
        remote(c_chip, c_z.at[d - 1], cz_s.at[d - 1], cz_r.at[d - 1], peer_z(d)) for d in range(1, n_z)
    ]
    for copy in c_second:
        copy.start()

    def correlate(i, carry):
        for d in range(n_z):
            gather_sib(i, d).wait()
        turned = samples_full[i].T
        gram[i] = dot(turned, samples_full[i], 1, 0) * (1.0 / order)
        for j in range(nj):
            raw[i, j] = dot(turned, left[i, j], 1, 0)
        return carry

    sib_copies2 = lambda i: remote(sib_send2.at[i], sib_recv2.at[i], fs_s.at[i], fs_r.at[i], sibling)
    z_copies2 = lambda i, d: remote(
        z_send2.at[i, d - 1], z_recv2.at[i, d - 1], fz_s.at[i, d - 1], fz_r.at[i, d - 1], peer_z(d)
    )

    def project(i, carry):
        for j in range(nj):
            turned = dot(inverse[i], raw[i, j], 1, 0, EXACT)
            reduced[j] = dot(coupling[i, j], turned, 1, 1, EXACT).astype(BF16)

        def rows_of(zz, inner):
            for parity in range(2):
                core = c if parity == 0 else 1 - c
                rows = row_block(2 * zz + core, rq)
                part = dot(left_full[0, rows, :], reduced[0], 1, 0)
                for j in range(1, nj):
                    part = part + dot(left_full[j, rows, :], reduced[j], 1, 0)
                if parity == 0:
                    acc[i, zz] = part
                else:
                    sib_send2[i, zz] = part.astype(BF16)
            return inner

        lax.fori_loop(0, n_z, rows_of, 0)
        sib_copies2(i).start()
        return carry

    def forward2(i, carry):
        sib_copies2(i).wait()
        for d in range(1, n_z):
            to = lax.rem(z + d, n_z)
            z_send2[i, d - 1] = (acc[i, to] + sib_recv2[i, to].astype(F32)).astype(BF16)
            z_copies2(i, d).start()
        return carry

    for start in range(0, ni, half):
        lax.fori_loop(start, start + half, relay, 0)
        lax.fori_loop(start, start + half, correlate, 0)
        inverse_factor(gram, eye, inverse, start, half, span, 32)
        if start == 0:
            for d in range(1, n_p):
                pl_copies[d - 1].wait()
            left_full[:, row_block(p, rp), :] = pivot_left[...]
        lax.fori_loop(start, start + half, project, 0)
        lax.fori_loop(start, start + half, forward2, 0)
    finish(c_second, c_chip, c_z, c_own, c_other, c_full, co_s, co_r)

    for i in range(ni):
        rows = pl.ds(i, rq, stride=ni)
        basis[rows, :] = dot(samples[i], -inverse[i], 1, 1, EXACT)
        turned = dot(inverse[i], c_full[i], 1, 0, EXACT).astype(BF16)
        value = dot(target_right[i], turned, 1, 1)
        value = value - acc[i, z] - sib_recv2[i, z].astype(F32)
        for d in range(1, n_z):
            z_copies2(i, d).wait()
            value = value - z_recv2[i, d - 1].astype(F32)
        coefficient[rows, :] = value

    @pl.when(p == owner)
    def _():
        for d in range(1, n_p):
            remote(probe.at[mine()], probe_block, probe_s.at[d - 1], probe_r, peer_p(d)).wait_send()


def per_device(
    n_p, n_q,
    left_factor, right_factor, pivot_left, pivot_right, target_left, target_right, probe, ranks,
):
    ni, nj, order, span = left_factor.shape
    rp = probe.shape[0]
    rq = target_left.shape[0]
    n_z = n_q // 2
    half = ni // 2
    square = (span, span)
    dma = pltpu.SemaphoreType.DMA
    one = dma(())
    z1 = max(n_z - 1, 1)
    p1 = max(n_p - 1, 1)

    def small(wire):
        return [
            pltpu.VMEM((ni,) + square, F32),
            pltpu.VMEM((half,) + square, F32),
            pltpu.VMEM((half,) + square, wire),
            pltpu.VMEM((z1, half) + square, wire),
            pltpu.VMEM((half,) + square, F32),
            pltpu.VMEM((half,) + square, F32),
            pltpu.VMEM((ni,) + square, F32),
        ]

    def exchange():
        return [
            pltpu.VMEM((ni, n_z, rq, span), BF16),
            pltpu.VMEM((ni, n_z, rq, span), BF16),
            pltpu.VMEM((ni, z1, rq, span), BF16),
            pltpu.VMEM((ni, z1, rq, span), BF16),
        ]

    scratch = [
        pltpu.SMEM((ni, nj), jnp.int32),
        pltpu.VMEM((ni, nj, order, span), BF16),
        pltpu.VMEM((ni, nj, order, span), BF16),
        pltpu.VMEM((nj, order, span), BF16),
        pltpu.VMEM((nj, order, span), BF16),
        pltpu.VMEM((rq, span), BF16),
        pltpu.VMEM((ni, nj) + square, F32),
        pltpu.VMEM((nj,) + square, BF16),
        pltpu.VMEM((nj,) + square, F32),
        pltpu.VMEM((p1, nj) + square, F32),
        pltpu.VMEM((nj,) + square, F32),
        *small(F32),
        pltpu.VMEM((ni, n_z, rq, span), F32),
        *exchange(),
        pltpu.VMEM((ni, rq, span), F32),
        pltpu.VMEM((ni, order, span), BF16),
        pltpu.VMEM((ni, nj) + square, F32),
        *small(BF16),
        pltpu.VMEM((ni,) + square, F32),
        pltpu.VMEM((ni,) + square, F32),
        pltpu.VMEM((ni,) + square, F32),
        pltpu.VMEM((nj,) + square, BF16),
        *exchange(),
        dma((3,)),
        dma((p1,)), one,
        dma((p1,)), dma((p1,)), dma((p1,)), dma((p1,)), dma((p1,)), dma((p1,)),
        one, one, dma((z1,)), dma((z1,)), one, one,
        dma((ni,)), dma((ni,)), dma((ni, z1)), dma((ni, z1)),
        dma((ni, z1)), dma((ni, z1)), dma((ni, n_z)), dma((ni, n_z)),
        one, one, dma((z1,)), dma((z1,)), one, one,
        dma((ni,)), dma((ni,)), dma((ni, z1)), dma((ni, z1)),
    ]
    vmem = pl.BlockSpec(memory_space=pltpu.VMEM)
    anywhere = pl.BlockSpec(memory_space=pl.ANY)
    out = jax.ShapeDtypeStruct((rq * ni, span), F32)
    basis, coefficient = pl.pallas_call(
        functools.partial(kernel, n_p, n_q),
        out_shape=(out, out),
        in_specs=[anywhere] * 2 + [vmem] * 5 + [anywhere],
        out_specs=(vmem, vmem),
        scratch_shapes=scratch,
        compiler_params=pltpu.CompilerParams(
            collective_id=0, has_side_effects=True, vmem_limit_bytes=56 * 1024 * 1024
        ),
    )(
        left_factor, right_factor, pivot_left, pivot_right,
        jnp.transpose(target_left, (1, 0, 2)), jnp.transpose(target_right, (1, 0, 2)), probe, ranks,
    )
    basis = jnp.negative(basis)
    coefficient = coefficient * (1.0 / order)
    return basis.reshape(rq, ni, span), coefficient.reshape(rq, ni, span)


def solution(mesh):
    in_specs = (
        P("prow", "pcol", None, None),
        P("prow", "pcol", None, None),
        P("pcol", "prow", None),
        P("pcol", "prow", None),
        P("pcol", "prow", None),
        P("pcol", "prow", None),
        P("prow", None),
        P("prow", "pcol"),
    )
    out_specs = (P("pcol", "prow", None), P("pcol", "prow", None))
    return jax.shard_map(
        functools.partial(per_device, mesh.shape["prow"], mesh.shape["pcol"]),
        mesh=mesh, in_specs=in_specs, out_specs=out_specs, check_vma=False,
    )
```

time: 351 us -> 135 us (0.38)
  waiting for transfers between devices: 154 us -> 0 us
  Pallas kernels: 0 us -> 127 us
  other arithmetic: 87.5 us -> 3.74 us
  blocking collectives: 49.1 us -> 0 us
  matrix products: 34.1 us -> 0 us
  between operations: 15.9 us -> 0.64 us
  local copies, waits for them, and re-layouts: 10.5 us -> 3.21 us
    pallas_call x0 -> x1, Pallas kernels: none -> 127 us  [per_device(): pl.pallas_call(functools.partial(kernel, n_p, n_q), out_shape=(out, out),...]
    psum x2 -> x0, waiting for transfers between devices: 96.3 us -> none  [the longest x1 95.5 us: per_device(): samples_all = lax.psum(partial_all, 'pcol')]
    another operation x7 -> x0, other arithmetic: 86.7 us -> none  [the longest x4 47.3 us: per_device(): lower_factor = jnp.linalg.cholesky(gram_matrix)]
    all_gather x2 -> x0, waiting for transfers between devices: 42.4 us -> none  [the longest x1 27.4 us: per_device(): lax.all_gather(pivot_right, 'prow', axis=1, tiled=True)]
    psum x1 -> x0, blocking collectives: 37.3 us -> none  [per_device(): target_correlation = lax.psum(correlation_part, 'pcol').astype(jnp.bfloat16)]
    dot_general x12 -> x0, matrix products: 25.2 us -> none  [the longest x1 7.4 us: per_device(): jnp.einsum('bir,bis->irs', samples_all, samples_all, precision=exact_mode)]
    reduce_scatter x1 -> x0, waiting for transfers between devices: 14.3 us -> none  [per_device(): lax.psum_scatter(-jnp.einsum('jbs,ijst->bit', pivot_whole, reduced, prefe...]
    all_gather x1 -> x0, blocking collectives: 11.8 us -> none  [per_device(): lax.all_gather(probe, 'prow', axis=0, tiled=True)]
  transfers between devices with their start and end apart: 5 -> 0, of which waited for: 5 -> 0; matrix products, arithmetic and copies ran while one was open for 5% -> 0% of each run, Pallas kernels for 0% -> 0%
where the time goes in v1:
time: 135 us; the launch traced here: 134 us
  Pallas kernels  127 us (94%)
  other arithmetic  3.74 us (3%)
  local copies, waits for them, and re-layouts  3.21 us (2%)
    pallas_call x1, Pallas kernels, per_device(): pl.pallas_call(functools.partial(kernel, n_p, n_q), out_shape=(out, out),...  127 us

profile of v1, /device:TPU:0, one launch (start us, length us, event | category | flops | bytes accessed | tf_op | source)
XLA Modules:
  0.0 134.3 jit_solution(8307632352410443997)
XLA Ops:
  0.6 1.3 copy.12.ranks_hbm
  1.9 1.9 %copy_bitcast_fusion = (bf16[4,256,128]{2,1,0:T(8,128)(2,1)}, bf16[4,256,128]{2,1,0:T(8,128)(2,1)}) fusion(bf16[256,4,128]{2,1,0:T(4,128)(2,1)} %param.13, bf16[256,4,128]{2,1,0:T(4,128)(2,1)} %param.12), kind=kLoop, calls=%fused_computation | loop fusion | bytes 1048576 | tf_op jit(solution)/shard_map/transpose | solution.py:447
  3.8 126.7 %shard_map.95 = (f32[1024,128]{1,0:T(8,128)}, f32[1024,128]{1,0:T(8,128)}) custom-call(bf16[4,2,2048,128]{3,2,1,0:T(8,128)(2,1)} %left_hbm.1, bf16[4,2,2048,128]{3,2,1,0:T(8,128)(2,1)} %right_hbm.1, bf16[2,512,128]{2,1,0:T(8,128)(2,1)} %pivot_left.1, bf16[2,512,128]{2,1,0:T(8,128)(2,1)} %pivot_right.1, bf16[4,256,128]{2,1,0:T(8,128)(2,1)} %get-tuple-element.7.target_left, ...), custom_call_target="tpu_custom_call" | custom-call | tf_op jit(solution)/shard_map/pallas_call | solution.py:436
  130.5 1.9 %neg.3 = f32[1024,128]{1,0:T(8,128)} negate(f32[1024,128]{1,0:T(8,128)} %get-tuple-element.4) | non-fusion elementwise | flops 131072 | bytes 1048576 | tf_op jit(solution)/shard_map/neg | solution.py:449
  132.4 1.9 %broadcast_multiply_fusion = f32[1024,128]{1,0:T(8,128)} fusion(f32[1024,128]{1,0:T(8,128)} %get-tuple-element.5), kind=kLoop, calls=%fused_computation.2 | loop fusion | flops 131072 | bytes 1048576 | tf_op jit(solution)/shard_map/mul | solution.py:450

commit v2 on v1

--- a/solution.py
+++ b/solution.py
@@ -58,17 +58,17 @@
     ranks, left, right, left_full, right_full, probe_block, coupling, weights,
     ps_part, ps_recv, ps_sum,
     t_part, t_sib, t_chip, t_z, t_own, t_other, t_full,
-    acc, sib_send, sib_recv, z_send, z_recv,
+    acc, sib_send, sib_recv, up_send, up_recv, down_send, down_recv,
     samples, samples_full, raw,
     c_part, c_sib, c_chip, c_z, c_own, c_other, c_full,
     gram, eye, inverse, reduced,
-    sib_send2, sib_recv2, z_send2, z_recv2,
+    sib_send2, sib_recv2, up_send2, up_recv2, down_send2, down_recv2,
     local_sem, probe_s, probe_r, pr_s, pr_r, ps_s, ps_r, pl_s, pl_r,
     ts_s, ts_r, tz_s, tz_r, to_s, to_r,
-    ss_s, ss_r, sz_s, sz_r,
-    gz_s, gz_r, gs_s, gs_r,
+    ss_s, ss_r, su_s, su_r, sd_s, sd_r,
+    gu_s, gu_r, gd_s, gd_r, gs_s, gs_r,
     cs_s, cs_r, cz_s, cz_r, co_s, co_r,
-    fs_s, fs_r, fz_s, fz_r,
+    fs_s, fs_r, fu_s, fu_r, fd_s, fd_r,
 ):
     p = lax.axis_index("prow")
     q = lax.axis_index("pcol")
@@ -183,10 +183,71 @@
     left_copy.wait()
     ranks_copy.wait()
 
+    above = (p, lax.rem(z + 1, n_z) * 2 + c)
+    beneath = (p, lax.rem(z + n_z - 1, n_z) * 2 + c)
+
+    def chain(siblings, got, u_send, u_recv, d_send, d_recv, us, ur, ds, dr):
+        def up(i, t):
+            return remote(u_send.at[i, t], u_recv.at[i, t], us.at[i, t], ur.at[i, t], above)
+
+        def down(i, t):
+            return remote(d_send.at[i, t], d_recv.at[i, t], ds.at[i, t], dr.at[i, t], beneath)
+
+        def add(i, carry):
+            siblings(i).wait()
+            for zz in range(n_z):
+                acc[i, zz] += got[i, zz].astype(F32)
+            return carry
+
+        lax.fori_loop(0, ni, add, 0)
+
+        def one_way(t, i, to, sends, first, copy, out, arrived):
+            @pl.when(sends)
+            def _():
+                @pl.when(first)
+                def _():
+                    out[i, t] = acc[i, to].astype(BF16)
+
+                @pl.when(jnp.logical_not(first))
+                def _():
+                    copy(i, t).wait_recv()
+                    out[i, t] = (acc[i, to] + arrived[i, t].astype(F32)).astype(BF16)
+
+                copy(i, t).start()
+
+        for t in range(n_z - 1):
+            def step(i, carry, t=t):
+                top = n_z - 1 - t
+                one_way(t, i, top, z < top, z == 0, up, u_send, u_recv)
+                one_way(t, i, t, z > t, z == n_z - 1, down, d_send, d_recv)
+                return carry
+
+            lax.fori_loop(0, ni, step, 0)
+
+        def finals(i, carry):
+            for t in range(n_z - 1):
+                @pl.when(z == n_z - 1 - t)
+                def _():
+                    up(i, t).wait_recv()
+                    acc[i, n_z - 1 - t] += u_recv[i, t].astype(F32)
+
+                @pl.when(z == t)
+                def _():
+                    down(i, t).wait_recv()
+                    acc[i, t] += d_recv[i, t].astype(F32)
+
+                @pl.when(z < n_z - 1 - t)
+                def _():
+                    up(i, t).wait_send()
+
+                @pl.when(z > t)
+                def _():
+                    down(i, t).wait_send()
+            return carry
+
+        lax.fori_loop(0, ni, finals, 0)
+
     sib_copies = lambda i: remote(sib_send.at[i], sib_recv.at[i], ss_s.at[i], ss_r.at[i], sibling)
-    z_copies = lambda i, d: remote(
-        z_send.at[i, d - 1], z_recv.at[i, d - 1], sz_s.at[i, d - 1], sz_r.at[i, d - 1], peer_z(d)
-    )
     lane = lax.broadcasted_iota(jnp.int32, (span, span), 1)
 
     def update(i, carry):
@@ -214,20 +275,7 @@
 
     lax.fori_loop(0, ni, update, 0)
 
-    def forward(i, carry):
-        sib_copies(i).wait()
-        for d in range(1, n_z):
-            to = lax.rem(z + d, n_z)
-            z_send[i, d - 1] = (acc[i, to] + sib_recv[i, to].astype(F32)).astype(BF16)
-            z_copies(i, d).start()
-        return carry
-
-    def sent(i, carry):
-        for d in range(1, n_z):
-            z_copies(i, d).wait_send()
-        return carry
-
-    lax.fori_loop(0, half, forward, 0)
+    chain(sib_copies, sib_recv, up_send, up_recv, down_send, down_recv, su_s, su_r, sd_s, sd_r)
 
     def finish(second, chip, arrived, own, other, whole, s, r):
         for copy in second:
@@ -243,43 +291,75 @@
         whole[half_of(1 - c)] = other[...]
 
     finish(t_second, t_chip, t_z, t_own, t_other, t_full, to_s, to_r)
-    lax.fori_loop(0, half, sent, 0)
-    lax.fori_loop(half, ni, forward, 0)
-
-    gather_z = lambda i, d: remote(
-        samples_full.at[i, row_block(q, rq), :], samples_full.at[i, row_block(q, rq), :],
-        gz_s.at[i, d - 1], gz_r.at[i, d - 1], peer_z(d),
-    )
-
-    def gather_sib(i, d):
-        rows = row_block(2 * lax.rem(z - d + n_z, n_z) + c, rq)
-        block = samples_full.at[i, rows, :]
-        return remote(block, block, gs_s.at[i, d], gs_r.at[i, d], sibling)
+
+    def gather(i, origin, t, s_sem, r_sem, where):
+        block = samples_full.at[i, row_block(2 * origin + c, rq), :]
+        return remote(block, block, s_sem.at[i, t], r_sem.at[i, t], where)
+
+    def wrap(index):
+        return lax.rem(index + n_z, n_z)
+
+    def gather_up(i, t):
+        return gather(i, wrap(z - t), t, gu_s, gu_r, above)
+
+    def gather_down(i, t):
+        return gather(i, wrap(z + t), t, gd_s, gd_r, beneath)
+
+    def gather_sib(i, origin):
+        block = samples_full.at[i, row_block(2 * origin + c, rq), :]
+        return remote(block, block, gs_s.at[i, origin], gs_r.at[i, origin], sibling)
 
     def sample(i, carry):
         value = dot(target_left[i].astype(F32), t_full[i], 1, 0, EXACT)
-        value = value - acc[i, z] - sib_recv[i, z].astype(F32)
-        for d in range(1, n_z):
-            z_copies(i, d).wait_recv()
-            value = value - z_recv[i, d - 1].astype(F32)
+        value = value - acc[i, z]
         samples[i] = value
         rounded = value.astype(BF16)
         samples_full[i, row_block(q, rq), :] = rounded
-        for d in range(1, n_z):
-            gather_z(i, d).start()
-        gather_sib(i, 0).start()
+        if n_z > 1:
+            @pl.when(z < n_z - 1)
+            def _():
+                gather_up(i, 0).start()
+
+            @pl.when(z > 0)
+            def _():
+                gather_down(i, 0).start()
+
+        gather_sib(i, z).start()
         c_part[i] = dot(rounded, target_left[i], 0, 0)
         return carry
 
     lax.fori_loop(0, ni, sample, 0)
-    lax.fori_loop(half, ni, sent, 0)
     c_first = remote(c_part.at[half_of(1 - c)], c_sib, cs_s, cs_r, sibling)
     c_first.start()
 
-    def relay(i, carry):
-        for d in range(1, n_z):
-            gather_z(i, d).wait()
-            gather_sib(i, d).start()
+    def relay(t, i):
+        @pl.when(z - 1 - t >= 0)
+        def _():
+            gather_up(i, t).wait_recv()
+            if t + 1 < n_z - 1:
+                @pl.when(z < n_z - 1)
+                def _():
+                    gather_up(i, t + 1).start()
+            gather_sib(i, wrap(z - 1 - t)).start()
+
+        @pl.when(z + 1 + t < n_z)
+        def _():
+            gather_down(i, t).wait_recv()
+            if t + 1 < n_z - 1:
+                @pl.when(z > 0)
+                def _():
+                    gather_down(i, t + 1).start()
+            gather_sib(i, wrap(z + 1 + t)).start()
+
+    def relayed(i, carry):
+        for t in range(n_z - 1):
+            @pl.when(jnp.logical_and(z < n_z - 1, z - t >= 0))
+            def _():
+                gather_up(i, t).wait_send()
+
+            @pl.when(jnp.logical_and(z > 0, z + t < n_z))
+            def _():
+                gather_down(i, t).wait_send()
         return carry
 
     c_first.wait()
@@ -291,8 +371,8 @@
         copy.start()
 
     def correlate(i, carry):
-        for d in range(n_z):
-            gather_sib(i, d).wait()
+        for origin in range(n_z):
+            gather_sib(i, origin).wait()
         turned = samples_full[i].T
         gram[i] = dot(turned, samples_full[i], 1, 0) * (1.0 / order)
         for j in range(nj):
@@ -300,10 +380,6 @@
         return carry
 
     sib_copies2 = lambda i: remote(sib_send2.at[i], sib_recv2.at[i], fs_s.at[i], fs_r.at[i], sibling)
-    z_copies2 = lambda i, d: remote(
-        z_send2.at[i, d - 1], z_recv2.at[i, d - 1], fz_s.at[i, d - 1], fz_r.at[i, d - 1], peer_z(d)
-    )
-
     def project(i, carry):
         for j in range(nj):
             turned = dot(inverse[i], raw[i, j], 1, 0, EXACT)
@@ -326,24 +402,20 @@
         sib_copies2(i).start()
         return carry
 
-    def forward2(i, carry):
-        sib_copies2(i).wait()
-        for d in range(1, n_z):
-            to = lax.rem(z + d, n_z)
-            z_send2[i, d - 1] = (acc[i, to] + sib_recv2[i, to].astype(F32)).astype(BF16)
-            z_copies2(i, d).start()
-        return carry
-
-    for start in range(0, ni, half):
-        lax.fori_loop(start, start + half, relay, 0)
-        lax.fori_loop(start, start + half, correlate, 0)
-        inverse_factor(gram, eye, inverse, start, half, span, 32)
-        if start == 0:
-            for d in range(1, n_p):
-                pl_copies[d - 1].wait()
-            left_full[:, row_block(p, rp), :] = pivot_left[...]
-        lax.fori_loop(start, start + half, project, 0)
-        lax.fori_loop(start, start + half, forward2, 0)
+    for t in range(n_z - 1):
+        def relay_all(i, carry, t=t):
+            relay(t, i)
+            return carry
+
+        lax.fori_loop(0, ni, relay_all, 0)
+    lax.fori_loop(0, ni, correlate, 0)
+    lax.fori_loop(0, ni, relayed, 0)
+    inverse_factor(gram, eye, inverse, 0, ni, span, 32)
+    for d in range(1, n_p):
+        pl_copies[d - 1].wait()
+    left_full[:, row_block(p, rp), :] = pivot_left[...]
+    lax.fori_loop(0, ni, project, 0)
+    chain(sib_copies2, sib_recv2, up_send2, up_recv2, down_send2, down_recv2, fu_s, fu_r, fd_s, fd_r)
     finish(c_second, c_chip, c_z, c_own, c_other, c_full, co_s, co_r)
 
     for i in range(ni):
@@ -351,10 +423,7 @@
         basis[rows, :] = dot(samples[i], -inverse[i], 1, 1, EXACT)
         turned = dot(inverse[i], c_full[i], 1, 0, EXACT).astype(BF16)
         value = dot(target_right[i], turned, 1, 1)
-        value = value - acc[i, z] - sib_recv2[i, z].astype(F32)
-        for d in range(1, n_z):
-            z_copies2(i, d).wait()
-            value = value - z_recv2[i, d - 1].astype(F32)
+        value = value - acc[i, z]
         coefficient[rows, :] = value
 
     @pl.when(p == owner)
@@ -393,6 +462,8 @@
         return [
             pltpu.VMEM((ni, n_z, rq, span), BF16),
             pltpu.VMEM((ni, n_z, rq, span), BF16),
+            pltpu.VMEM((ni, z1, rq, span), BF16),
+            pltpu.VMEM((ni, z1, rq, span), BF16),
             pltpu.VMEM((ni, z1, rq, span), BF16),
             pltpu.VMEM((ni, z1, rq, span), BF16),
         ]
@@ -425,10 +496,10 @@
         dma((p1,)), one,
         dma((p1,)), dma((p1,)), dma((p1,)), dma((p1,)), dma((p1,)), dma((p1,)),
         one, one, dma((z1,)), dma((z1,)), one, one,
-        dma((ni,)), dma((ni,)), dma((ni, z1)), dma((ni, z1)),
-        dma((ni, z1)), dma((ni, z1)), dma((ni, n_z)), dma((ni, n_z)),
+        dma((ni,)), dma((ni,)), dma((ni, z1)), dma((ni, z1)), dma((ni, z1)), dma((ni, z1)),
+        dma((ni, z1)), dma((ni, z1)), dma((ni, z1)), dma((ni, z1)), dma((ni, n_z)), dma((ni, n_z)),
         one, one, dma((z1,)), dma((z1,)), one, one,
-        dma((ni,)), dma((ni,)), dma((ni, z1)), dma((ni, z1)),
+        dma((ni,)), dma((ni,)), dma((ni, z1)), dma((ni, z1)), dma((ni, z1)), dma((ni, z1)),
     ]
     vmem = pl.BlockSpec(memory_space=pltpu.VMEM)
     anywhere = pl.BlockSpec(memory_space=pl.ANY)

time: 135 us -> 165 us (1.22)
  Pallas kernels: 127 us -> 156 us
    pallas_call x1, Pallas kernels: 127 us -> 156 us  [per_device(): pl.pallas_call(functools.partial(kernel, n_p, n_q), out_shape=(out, out),...]
where the time goes in v2:
time: 165 us; the launch traced here: 164 us
  Pallas kernels  156 us (95%)
  other arithmetic  3.74 us (2%)
  local copies, waits for them, and re-layouts  3.21 us (2%)
    pallas_call x1, Pallas kernels, per_device(): pl.pallas_call(functools.partial(kernel, n_p, n_q), out_shape=(out, out),...  156 us

profile of v2, /device:TPU:0, one launch (start us, length us, event | category | flops | bytes accessed | tf_op | source)
XLA Modules:
  0.0 163.6 jit_solution(10495218588760470557)
XLA Ops:
  0.6 1.3 copy.12.ranks_hbm
  1.9 1.9 %copy_bitcast_fusion = (bf16[4,256,128]{2,1,0:T(8,128)(2,1)}, bf16[4,256,128]{2,1,0:T(8,128)(2,1)}) fusion(bf16[256,4,128]{2,1,0:T(4,128)(2,1)} %param.13, bf16[256,4,128]{2,1,0:T(4,128)(2,1)} %param.12), kind=kLoop, calls=%fused_computation | loop fusion | bytes 1048576 | tf_op jit(solution)/shard_map/transpose | solution.py:518
  3.8 156.0 %shard_map.95 = (f32[1024,128]{1,0:T(8,128)}, f32[1024,128]{1,0:T(8,128)}) custom-call(bf16[4,2,2048,128]{3,2,1,0:T(8,128)(2,1)} %left_hbm.1, bf16[4,2,2048,128]{3,2,1,0:T(8,128)(2,1)} %right_hbm.1, bf16[2,512,128]{2,1,0:T(8,128)(2,1)} %pivot_left.1, bf16[2,512,128]{2,1,0:T(8,128)(2,1)} %pivot_right.1, bf16[4,256,128]{2,1,0:T(8,128)(2,1)} %get-tuple-element.7.target_left, ...), custom_call_target="tpu_custom_call" | custom-call | tf_op jit(solution)/shard_map/pallas_call | solution.py:507
  159.8 1.9 %neg.3 = f32[1024,128]{1,0:T(8,128)} negate(f32[1024,128]{1,0:T(8,128)} %get-tuple-element.4) | non-fusion elementwise | flops 131072 | bytes 1048576 | tf_op jit(solution)/shard_map/neg | solution.py:520
  161.7 1.9 %broadcast_multiply_fusion = f32[1024,128]{1,0:T(8,128)} fusion(f32[1024,128]{1,0:T(8,128)} %get-tuple-element.5), kind=kLoop, calls=%fused_computation.2 | loop fusion | flops 131072 | bytes 1048576 | tf_op jit(solution)/shard_map/mul | solution.py:521

commit v3 on v1

--- a/solution.py
+++ b/solution.py
@@ -156,7 +156,7 @@
             i, j = n // nj, n % nj
             coupling[i, j] += dot(chunk_ref[j], right[i, j, rows, :], 0, 0)
             return carry
-        lax.fori_loop(0, ni * nj, body, 0)
+        lax.fori_loop(0, ni * nj, body, 0, unroll=True)
 
     coupling[...] = jnp.zeros_like(coupling)
     couple(row_block(p, rp), pivot_right)
@@ -189,26 +189,27 @@
     )
     lane = lax.broadcasted_iota(jnp.int32, (span, span), 1)
 
-    def update(i, carry):
+    for i in range(ni):
         for j in range(nj):
             masked = jnp.where(lane < ranks[i, j], coupling[i, j], 0.0)
             coupling[i, j] = masked
-            weights[j] = dot(masked.T, ps_sum[j], 1, 0, EXACT).astype(BF16)
-
+            weights[i, j] = dot(masked.T, ps_sum[j], 1, 0, EXACT).astype(BF16)
+
+    def update(i, carry):
         def rows_of(zz, inner):
             for parity in range(2):
                 core = c if parity == 0 else 1 - c
                 rows = row_block(2 * zz + core, rq)
-                part = dot(left[i, 0, rows, :], weights[0], 1, 0)
+                part = dot(left[i, 0, rows, :], weights[i, 0], 1, 0)
                 for j in range(1, nj):
-                    part = part + dot(left[i, j, rows, :], weights[j], 1, 0)
+                    part = part + dot(left[i, j, rows, :], weights[i, j], 1, 0)
                 if parity == 0:
                     acc[i, zz] = part
                 else:
                     sib_send[i, zz] = part.astype(BF16)
             return inner
 
-        lax.fori_loop(0, n_z, rows_of, 0)
+        lax.fori_loop(0, n_z, rows_of, 0, unroll=True)
         sib_copies(i).start()
         return carry
 
@@ -304,25 +305,27 @@
         z_send2.at[i, d - 1], z_recv2.at[i, d - 1], fz_s.at[i, d - 1], fz_r.at[i, d - 1], peer_z(d)
     )
 
+    def reduce(start):
+        pairs = [(i, j) for i in range(start, start + half) for j in range(nj)]
+        turned = [dot(inverse[i], raw[i, j], 1, 0, EXACT) for i, j in pairs]
+        for (i, j), value in zip(pairs, turned):
+            reduced[i, j] = dot(coupling[i, j], value, 1, 1, EXACT).astype(BF16)
+
     def project(i, carry):
-        for j in range(nj):
-            turned = dot(inverse[i], raw[i, j], 1, 0, EXACT)
-            reduced[j] = dot(coupling[i, j], turned, 1, 1, EXACT).astype(BF16)
-
         def rows_of(zz, inner):
             for parity in range(2):
                 core = c if parity == 0 else 1 - c
                 rows = row_block(2 * zz + core, rq)
-                part = dot(left_full[0, rows, :], reduced[0], 1, 0)
+                part = dot(left_full[0, rows, :], reduced[i, 0], 1, 0)
                 for j in range(1, nj):
-                    part = part + dot(left_full[j, rows, :], reduced[j], 1, 0)
+                    part = part + dot(left_full[j, rows, :], reduced[i, j], 1, 0)
                 if parity == 0:
                     acc[i, zz] = part
                 else:
                     sib_send2[i, zz] = part.astype(BF16)
             return inner
 
-        lax.fori_loop(0, n_z, rows_of, 0)
+        lax.fori_loop(0, n_z, rows_of, 0, unroll=True)
         sib_copies2(i).start()
         return carry
 
@@ -336,12 +339,13 @@
 
     for start in range(0, ni, half):
         lax.fori_loop(start, start + half, relay, 0)
-        lax.fori_loop(start, start + half, correlate, 0)
+        lax.fori_loop(start, start + half, correlate, 0, unroll=True)
         inverse_factor(gram, eye, inverse, start, half, span, 32)
         if start == 0:
             for d in range(1, n_p):
                 pl_copies[d - 1].wait()
             left_full[:, row_block(p, rp), :] = pivot_left[...]
+        reduce(start)
         lax.fori_loop(start, start + half, project, 0)
         lax.fori_loop(start, start + half, forward2, 0)
     finish(c_second, c_chip, c_z, c_own, c_other, c_full, co_s, co_r)
@@ -405,7 +409,7 @@
         pltpu.VMEM((nj, order, span), BF16),
         pltpu.VMEM((rq, span), BF16),
         pltpu.VMEM((ni, nj) + square, F32),
-        pltpu.VMEM((nj,) + square, BF16),
+        pltpu.VMEM((ni, nj) + square, BF16),
         pltpu.VMEM((nj,) + square, F32),
         pltpu.VMEM((p1, nj) + square, F32),
         pltpu.VMEM((nj,) + square, F32),
@@ -419,7 +423,7 @@
         pltpu.VMEM((ni,) + square, F32),
         pltpu.VMEM((ni,) + square, F32),
         pltpu.VMEM((ni,) + square, F32),
-        pltpu.VMEM((nj,) + square, BF16),
+        pltpu.VMEM((ni, nj) + square, BF16),
         *exchange(),
         dma((3,)),
         dma((p1,)), one,

time: 135 us -> 130 us (0.963)
  Pallas kernels: 127 us -> 123 us
    pallas_call x1, Pallas kernels: 127 us -> 123 us  [per_device(): pl.pallas_call(functools.partial(kernel, n_p, n_q), out_shape=(out, out),...]
where the time goes in v3:
time: 130 us
  Pallas kernels  123 us (95%)
  other arithmetic  3.74 us (3%)
  local copies, waits for them, and re-layouts  3.21 us (2%)
    pallas_call x1, Pallas kernels, per_device(): pl.pallas_call(functools.partial(kernel, n_p, n_q), out_shape=(out, out),...  123 us

profile of v3, /device:TPU:0, one launch (start us, length us, event | category | flops | bytes accessed | tf_op | source)
XLA Modules:
  0.0 130.1 jit_solution(5703841208557124152)
XLA Ops:
  0.6 1.3 %copy.12.ranks_hbm = s32[4,2]{1,0:T(4,128)} copy(s32[4,2]{0,1:T(2,128)} %param.15) | data formatting | bytes 64 | tf_op args[7]
  1.9 1.9 %copy_bitcast_fusion = (bf16[4,256,128]{2,1,0:T(8,128)(2,1)}, bf16[4,256,128]{2,1,0:T(8,128)(2,1)}) fusion(bf16[256,4,128]{2,1,0:T(4,128)(2,1)} %param.13, bf16[256,4,128]{2,1,0:T(4,128)(2,1)} %param.12), kind=kLoop, calls=%fused_computation | loop fusion | bytes 1048576 | tf_op jit(solution)/shard_map/transpose | solution.py:451
  3.8 122.5 %shard_map.95 = (f32[1024,128]{1,0:T(8,128)}, f32[1024,128]{1,0:T(8,128)}) custom-call(bf16[4,2,2048,128]{3,2,1,0:T(8,128)(2,1)} %left_hbm.1, bf16[4,2,2048,128]{3,2,1,0:T(8,128)(2,1)} %right_hbm.1, bf16[2,512,128]{2,1,0:T(8,128)(2,1)} %pivot_left.1, bf16[2,512,128]{2,1,0:T(8,128)(2,1)} %pivot_right.1, bf16[4,256,128]{2,1,0:T(8,128)(2,1)} %get-tuple-element.7.target_left, ...), custom_call_target="tpu_custom_call" | custom-call | tf_op jit(solution)/shard_map/pallas_call | solution.py:440
  126.4 1.9 %neg.3 = f32[1024,128]{1,0:T(8,128)} negate(f32[1024,128]{1,0:T(8,128)} %get-tuple-element.4) | non-fusion elementwise | flops 131072 | bytes 1048576 | tf_op jit(solution)/shard_map/neg | solution.py:453
  128.2 1.9 %broadcast_multiply_fusion = f32[1024,128]{1,0:T(8,128)} fusion(f32[1024,128]{1,0:T(8,128)} %get-tuple-element.5), kind=kLoop, calls=%fused_computation.2 | loop fusion | flops 131072 | bytes 1048576 | tf_op jit(solution)/shard_map/mul | solution.py:454
